TPU v7x, 256 devices: a whole 4x4x8 slice. The times are simulated.
256 devices in a mesh: dp: 64 (over x, z, core), feat: 4 (over y).
Axes of the slice: x: 4, y: 4, z: 8, core: 2. Of those that a mesh axis runs over, the one named last changes fastest.
Arguments:
- training_grads: bfloat16 [65536, 8192], P('dp', 'feat'), may hold values from -6 to 6
- validation_grads: bfloat16 [1024, 8192], P('dp', 'feat'), may hold values from -6 to 6
- test_matrix: bfloat16 [65536, 256], P('dp'), may hold values from -0.0234375 to 0.0234375
Outputs:
- scores: float32 [1024, 65536], P(None, ('dp', 'feat'))
All inputs are finite; a program needn't handle non-finite values.
Results may differ from a plain program's by a relative error of at most 0.0038.
Values may be sent and summed in bfloat16 or wider, within the bound.
No kernel may reach another device: no remote copies, remote signals or barrier semaphores. Data moves between devices by JAX's collectives and lax.ppermute only.
A program may use at most 64 MiB of HBM per device.

v0:
```python
import math

import jax
import jax.numpy as jnp
from jax import lax
from jax.sharding import PartitionSpec as P

damping = 0.1


def local(training_grads, validation_grads, test_matrix):
    highest = lax.Precision.HIGHEST
    row_count, local_width = training_grads.shape
    rank_size = test_matrix.shape[1]
    val_block = lax.all_gather(validation_grads, "dp", axis=0, tiled=True)
    partial_basis = lax.dot_general(
        training_grads, test_matrix, (((0,), (0,)), ((), ())), preferred_element_type=jnp.float32
    )
    basis_raw = lax.psum(partial_basis, "dp")
    basis_gram = lax.psum(jnp.dot(basis_raw.T, basis_raw, precision=highest), "feat")
    factor = jnp.linalg.cholesky(basis_gram)
    basis = jax.scipy.linalg.solve_triangular(factor, basis_raw.T, lower=True).T.astype(
        jnp.bfloat16
    )
    train_part = jnp.dot(training_grads, basis, preferred_element_type=jnp.float32)
    val_part = jnp.dot(val_block, basis, preferred_element_type=jnp.float32)
    total_train = row_count * lax.axis_size("dp")
    train_coords, val_summed = lax.psum((train_part, val_part), "feat")
    curvature = (
        lax.psum(jnp.dot(train_coords.T, train_coords, precision=highest), "dp") / total_train
    )
    quarter = row_count // lax.axis_size("feat")
    mine = lax.dynamic_slice_in_dim(train_coords, lax.axis_index("feat") * quarter, quarter, 0)
    curvature = curvature + damping * jnp.eye(rank_size, dtype=jnp.float32)
    curv_factor = jnp.linalg.cholesky(curvature)
    solved = jax.scipy.linalg.cho_solve((curv_factor, True), val_summed.T)
    return jnp.dot(solved.T, mine.T, precision=highest) / math.sqrt(rank_size)


def solution(mesh):
    in_specs = (P("dp", "feat"), P("dp", "feat"), P("dp", None))
    out_specs = P(None, ("dp", "feat"))
    return jax.shard_map(local, mesh=mesh, in_specs=in_specs, out_specs=out_specs, check_vma=False)
```

profile of v0, /device:TPU:1, one launch (start us, length us, event | category | flops | bytes accessed | tf_op | source)
XLA Modules:
  0.0 663.3 jit_solution(10377500827558147527)
XLA Ops:
  7.6 4.8 fusion.34
  12.5 191.6 %all-reduce.7.cloned.1.call-done = f32[2048,256]{1,0:T(8,128)} async-done(((f32[2048,256]{1,0:T(8,128)}), f32[2048,256]{1,0:T(8,128)}) %all-reduce.7.cloned.1.call-update) | async-done | bytes 2097168 | tf_op jit(solution)/shard_map/psum | solution.py:19
  204.1 6.4 fusion.35
  211.6 44.1 %all-reduce.9.cloned.1.call-done = f32[256,256]{0,1:T(8,128)} async-done(((f32[256,256]{0,1:T(8,128)}), f32[256,256]{0,1:T(8,128)}) %all-reduce.9.cloned.1.call-update) | async-done | bytes 262160 | tf_op jit(solution)/shard_map/psum | solution.py:20
  257.8 11.7 %cholesky.130 = f32[128,128]{1,0:T(8,128)S(1)} custom-call(f32[128,128]{1,0:T(8,128)S(1)} %cholesky.194), custom_call_target="Cholesky" | custom-call | tf_op jit(solution)/shard_map/jit(cholesky)/cholesky | solution.py:21
  269.7 9.8 %custom-call.22 = f32[1,128,128]{1,2,0:T(8,128)S(1)} custom-call(f32[1,128,128]{2,1,0:T(8,128)S(1)} %get-tuple-element.55), custom_call_target="InvertDiagBlocksLowerTriangular" | custom-call | tf_op jit(solution)/shard_map/jit(cholesky)/cholesky | solution.py:21
  280.1 11.7 %cholesky.147 = f32[128,128]{1,0:T(8,128)S(1)} custom-call(f32[128,128]{1,0:T(8,128)S(1)} %convolution_subtract_fusion.4), custom_call_target="Cholesky" | custom-call | tf_op jit(solution)/shard_map/jit(cholesky)/cholesky | solution.py:21
  294.0 4.6 while.2
  298.6 19.7 %custom-call.19 = f32[2,128,128]{1,2,0:T(8,128)S(1)} custom-call(f32[2,128,128]{2,1,0:T(8,128)S(1)} %get-tuple-element.13), custom_call_target="InvertDiagBlocksLowerTriangular" | custom-call | tf_op jit(solution)/shard_map/jit(_solve_triangular)/triangular_solve | solution.py:22
  319.4 1.8 convolution_subtract_fusion
  322.3 2.3 convolution_bitcast_fusion
  324.6 16.9 %all-gather.2.cloned.1.call-done = bf16[1024,2048]{1,0:T(8,128)(2,1)} async-done(((bf16[16,2048]{1,0:T(8,128)(2,1)}), bf16[1024,2048]{1,0:T(8,128)(2,1)}) %all-gather.2.cloned.1.call-update) | async-done | bytes 4194320 | tf_op jit(solution)/shard_map/all_gather | solution.py:15
  341.5 4.4 fusion.5
  346.2 61.1 %all-reduce.13.cloned.1.call-done = (f32[256,1024]{1,0:T(8,128)}, f32[1024,256]{0,1:T(8,128)}) async-done(((f32[256,1024]{1,0:T(8,128)}, f32[1024,256]{0,1:T(8,128)}), (f32[256,1024]{1,0:T(8,128)}, f32[1024,256]{0,1:T(8,128)})) %all-reduce.13.cloned.1.call-update) | async-done | bytes 2097168 | tf_op jit(solution)/shard_map/psum | solution.py:28
  407.3 3.4 fusion.36
  410.7 175.4 %all-reduce.11.cloned.1.call-done = f32[256,256]{0,1:T(8,128)} async-done(((f32[256,256]{0,1:T(8,128)}), f32[256,256]{0,1:T(8,128)}) %all-reduce.11.cloned.1.call-update) | async-done | bytes 262160 | tf_op jit(solution)/shard_map/psum | solution.py:30
  588.2 11.7 %cholesky.164 = f32[128,128]{1,0:T(8,128)S(1)} custom-call(f32[128,128]{1,0:T(8,128)S(1)} %cholesky.197), custom_call_target="Cholesky" | custom-call | tf_op jit(solution)/shard_map/jit(cholesky)/cholesky | solution.py:35
  600.0 9.8 %custom-call.23 = f32[1,128,128]{1,2,0:T(8,128)S(1)} custom-call(f32[1,128,128]{2,1,0:T(8,128)S(1)} %get-tuple-element.53), custom_call_target="InvertDiagBlocksLowerTriangular" | custom-call | tf_op jit(solution)/shard_map/jit(cholesky)/cholesky | solution.py:35
  610.3 11.7 %cholesky.181 = f32[128,128]{1,0:T(8,128)S(1)} custom-call(f32[128,128]{1,0:T(8,128)S(1)} %convolution_subtract_fusion.3), custom_call_target="Cholesky" | custom-call | tf_op jit(solution)/shard_map/jit(cholesky)/cholesky | solution.py:35
  625.0 4.4 while.3
  625.8 1.4 dynamic-slice.15
  627.9 1.4 dynamic-slice.15
  629.4 19.7 %custom-call.20 = f32[2,128,128]{1,2,0:T(8,128)S(1)} custom-call(f32[2,128,128]{2,1,0:T(8,128)S(1)} %get-tuple-element.21), custom_call_target="InvertDiagBlocksLowerTriangular" | custom-call | tf_op jit(solution)/shard_map/jit(_cho_solve)/triangular_solve | solution.py:36
  652.8 3.7 convolution_multiply_fusion
  (80 shorter events, 21.6 us)
Async XLA Ops:
  6.5 1.0 copy-start
  6.5 197.6 %all-reduce.7.cloned.1.call-start = ((), (), s32[]{:S(2)}) async-start(), calls=%async_computation | async-start | bytes 4194304 | tf_op jit(solution)/shard_map/psum | solution.py:19
  12.4 243.3 %all-reduce.9.cloned.1.call-start = ((), (), s32[]{:S(2)}) async-start(), calls=%async_computation.1 | async-start | bytes 524288 | tf_op jit(solution)/shard_map/psum | solution.py:20
  210.5 131.0 %all-gather.2.cloned.1.call-start = ((), (), s32[]{:S(2)}) async-start(), calls=%async_computation.3 | async-start | bytes 4259840 | tf_op jit(solution)/shard_map/all_gather | solution.py:15
  211.3 196.0 %all-reduce.13.cloned.1.call-start = ((), (), s32[]{:S(2)}) async-start(), calls=%async_computation.4 | async-start | bytes 4194304 | tf_op jit(solution)/shard_map/psum | solution.py:28
  279.5 38.8 %copy-start.1 = (f32[2048,256]{1,0:T(8,128)S(1)}, f32[2048,256]{1,0:T(8,128)}, u32[]{:S(2)}) copy-start(f32[2048,256]{1,0:T(8,128)} %all-reduce.7.cloned.1.call-done) | copy-start | bytes 6291460
  319.4 2.9 copy-start.3
  345.9 240.2 %all-reduce.11.cloned.1.call-start = ((), (), s32[]{:S(2)}) async-start(), calls=%async_computation.2 | async-start | bytes 524288 | tf_op jit(solution)/shard_map/psum | solution.py:30
  610.0 39.1 %copy-start.2 = (f32[256,1024]{1,0:T(8,128)S(1)}, f32[256,1024]{1,0:T(8,128)}, u32[]{:S(2)}) copy-start(f32[256,1024]{1,0:T(8,128)} %get-tuple-element.46) | copy-start | bytes 3145732
Sparse Core Ops, SparseCore 0:
  12.6 191.4 all-reduce.6
  210.6 45.0 all-reduce.8
  258.9 82.5 all-gather.1
  346.1 61.1 all-reduce.12
  410.8 175.2 all-reduce.10
where the time goes:
time: 668 us; the launch traced here: 663 us
  waiting for transfers between devices  490 us (73%)
  other arithmetic  111 us (17%)
  matrix products  33.6 us (5%)
  between operations  16.2 us (2%)
  local copies, waits for them, and re-layouts  11.1 us (2%)
    psum x1, waiting for transfers between devices, local(): basis_raw = lax.psum(partial_basis, 'dp')  192 us
    psum x1, waiting for transfers between devices, local(): lax.psum(jnp.dot(train_coords.T, train_coords, precision=highest), 'dp')  175 us
    psum x1, waiting for transfers between devices, local(): train_coords, val_summed = lax.psum((train_part, val_part), 'feat')  61.1 us
    psum x1, waiting for transfers between devices, local(): lax.psum(jnp.dot(basis_raw.T, basis_raw, precision=highest), 'feat')  44.1 us
    another operation x7, other arithmetic, local(): curv_factor = jnp.linalg.cholesky(curvature)  34.6 us
    another operation x6, other arithmetic, local(): factor = jnp.linalg.cholesky(basis_gram)  34 us
    another operation x3, other arithmetic, local(): jax.scipy.linalg.solve_triangular(factor, basis_raw.T, lower=True)  19.7 us
    another operation x2, other arithmetic, local(): solved = jax.scipy.linalg.cho_solve((curv_factor, True), val_summed.T)  19.7 us
  transfers between devices with their start and end apart: 5, of which 5 were waited for; matrix products, arithmetic and copies ran while one was open for 10% of the time, Pallas kernels for 0%

commit v1 on v0

v1 whole, which is shorter than its diff:
```python
import math

import jax
import jax.numpy as jnp
from jax import lax
from jax.sharding import Mesh, PartitionSpec as P

damping = 0.1
f32 = jnp.float32


def scatter_sum(value, axis, size):
    rows = value.shape[0] // size
    parts = lax.all_to_all(value, axis, 0, 0, tiled=True)
    return jnp.sum(parts.reshape(size, rows, value.shape[1]), axis=0)


def gather(value, axis, size):
    copies = jnp.broadcast_to(value[None], (size,) + value.shape)
    rows = copies.reshape(size * value.shape[0], value.shape[1])
    return lax.all_to_all(rows, axis, 0, 0, tiled=True)


def local(sizes, training_grads, validation_grads, test_matrix):
    highest = lax.Precision.HIGHEST
    every = ("x", "z", "c", "y")
    devices = math.prod(sizes.values())
    row_count = training_grads.shape[0]
    rank_size = test_matrix.shape[1]
    total_train = row_count * devices // sizes["y"]
    with jax.named_scope("val_gather"):
        val_block = lax.all_gather(validation_grads, ("x", "z", "c"), axis=0, tiled=True)
    with jax.named_scope("raw_basis"):
        partial_basis = lax.dot_general(
            training_grads, test_matrix, (((0,), (0,)), ((), ())), preferred_element_type=f32
        )
        basis_rows = partial_basis
        for axis in ("c", "x", "z"):
            basis_rows = scatter_sum(basis_rows, axis, sizes[axis])
        basis = basis_rows.astype(jnp.bfloat16)
        for axis in ("z", "x", "c"):
            basis = gather(basis, axis, sizes[axis])
    with jax.named_scope("coords"):
        val_part = jnp.dot(val_block, basis, preferred_element_type=f32)
        val_coords = lax.psum(val_part, "y")
        train_part = jnp.dot(training_grads, basis, preferred_element_type=f32)
        mine = scatter_sum(train_part, "y", sizes["y"])
    with jax.named_scope("curvature"):
        stacked = jnp.concatenate(
            [mine * (1.0 / math.sqrt(total_train)), basis_rows * math.sqrt(damping)], axis=0
        )
        part = lax.dot_general(
            stacked, stacked, (((0,), (0,)), ((), ())), precision=highest, preferred_element_type=f32
        )
        part = part.reshape(devices, 2, 128)
        parts = lax.all_to_all(part, every, 0, 0, tiled=True)
        row = jnp.sum(parts, axis=0)
        copies = jnp.broadcast_to(row[None], (devices, 2, 128))
        curvature = lax.all_to_all(copies, every, 0, 0, tiled=True).reshape(rank_size, rank_size)
    with jax.named_scope("solve"):
        curv_factor = jnp.linalg.cholesky(curvature)
        solved = jax.scipy.linalg.cho_solve((curv_factor, True), mine.T)
    return jnp.dot(val_coords, solved, precision=highest) / math.sqrt(rank_size)


def solution(mesh):
    sizes = {"x": 4, "z": 8, "c": 2, "y": 4}
    split = Mesh(mesh.devices.reshape(tuple(sizes.values())), tuple(sizes))
    dp = ("x", "z", "c")

    def run(training_grads, validation_grads, test_matrix):
        return jax.shard_map(
            lambda *args: local(sizes, *args),
            mesh=split,
            in_specs=(P(dp, "y"), P(dp, "y"), P(dp, None)),
            out_specs=P(None, dp + ("y",)),
            check_vma=False,
        )(training_grads, validation_grads, test_matrix)

    return run
```

time: 668 us -> 276 us (0.41)
  waiting for transfers between devices: 490 us -> 72.2 us
  blocking collectives: 0 us -> 99.7 us
  other arithmetic: 111 us -> 55.4 us
  matrix products: 33.6 us -> 16.1 us
  starting transfers between devices: 0.63 us -> 9.82 us
    psum x4 -> x1, waiting for transfers between devices: 472 us -> 41.5 us  [local(): val_coords = lax.psum(val_part, 'y')]
    all_to_all x0 -> x7, blocking collectives: none -> 99.7 us  [the longest x3 43 us: scatter_sum(): parts = lax.all_to_all(value, axis, 0, 0, tiled=True)]
    another operation x11 -> x3, other arithmetic: 73.4 us -> 19.7 us  [local(): solved = jax.scipy.linalg.cho_solve((curv_factor, True), mine.T)]
    all_to_all x0 -> x2, waiting for transfers between devices: none -> 30 us  [the longest x1 15.6 us: local(): lax.all_to_all(copies, every, 0, 0, tiled=True)]
    all_gather x1, waiting for transfers between devices: 16.9 us -> 0.02 us  [local(): lax.all_gather(validation_grads, ('x', 'z', 'c'), axis=0, tiled=True)]
    dot_general x5 -> x4, matrix products: 20.2 us -> 10.4 us  [the longest x1 4.46 us: local(): val_part = jnp.dot(val_block, basis, preferred_element_type=f32)]
    all_to_all x0 -> x2, starting transfers between devices: none -> 9.6 us  [the longest x1 5.68 us: local(): lax.all_to_all(copies, every, 0, 0, tiled=True)]
    another operation x7 -> x6, other arithmetic: 34.6 us -> 34 us  [local(): curv_factor = jnp.linalg.cholesky(curvature)]
  transfers between devices with their start and end apart: 5 -> 4, of which waited for: 5 -> 3; matrix products, arithmetic and copies ran while one was open for 10% -> 25% of each run, Pallas kernels for 0% -> 0%
where the time goes in v1:
time: 276 us; the launch traced here: 275 us
  blocking collectives  99.7 us (36%)
  waiting for transfers between devices  72.2 us (26%)
  other arithmetic  55.4 us (20%)
  matrix products  16.1 us (6%)
  between operations  14.9 us (5%)
  starting transfers between devices  9.82 us (4%)
  local copies, waits for them, and re-layouts  6.74 us (2%)
    all_to_all x3, blocking collectives, scatter_sum(): parts = lax.all_to_all(value, axis, 0, 0, tiled=True)  43 us
    psum x1, waiting for transfers between devices, local(): val_coords = lax.psum(val_part, 'y')  41.5 us
    another operation x6, other arithmetic, local(): curv_factor = jnp.linalg.cholesky(curvature)  34 us
    all_to_all x3, blocking collectives, gather(): return lax.all_to_all(rows, axis, 0, 0, tiled=True)  32.7 us
    all_to_all x1, blocking collectives, local(): parts = lax.all_to_all(part, every, 0, 0, tiled=True)  24 us
    another operation x3, other arithmetic, local(): solved = jax.scipy.linalg.cho_solve((curv_factor, True), mine.T)  19.7 us
    all_to_all x1, waiting for transfers between devices, local(): lax.all_to_all(copies, every, 0, 0, tiled=True)  15.6 us
    all_to_all x1, waiting for transfers between devices, scatter_sum(): parts = lax.all_to_all(value, axis, 0, 0, tiled=True)  14.4 us
  transfers between devices with their start and end apart: 4, of which 3 were waited for; matrix products, arithmetic and copies ran while one was open for 25% of the time, Pallas kernels for 0%

profile of v1, /device:TPU:1, one launch (start us, length us, event | category | flops | bytes accessed | tf_op | source)
XLA Modules:
  0.0 275.2 jit_solution(3491975223309562823)
XLA Ops:
  7.6 3.5 %fusion.21 = f32[2048,256]{1,0:T(8,128)S(1)} fusion(bf16[1024,2048]{1,0:T(8,128)(2,1)} %param.3, bf16[1024,256]{1,0:T(8,128)(2,1)S(1)} %copy-done), kind=kOutput, calls=%fused_computation.46 | convolution fusion | flops 1073741824 | bytes 6815744 | tf_op jit(solution)/shard_map/raw_basis/dot_general | solution.py:34
  11.1 8.3 %all_to_all.67 = f32[2,1024,256]{2,1,0:T(8,128)S(1)} all-to-all(f32[2,1024,256]{2,1,0:T(8,128)S(1)} %bitcast.65), channel_id=1, replica_groups=mesh['x'=4,'z'=8,'c'=2,'y'=4] {'c'}, dimensions={0} | all-to-all | bytes 4194304 | tf_op jit(solution)/shard_map/raw_basis/all_to_all | solution.py:14
  19.4 1.2 reduce_sum.45
  20.6 19.1 %all_to_all.68 = f32[4,256,256]{2,1,0:T(8,128)S(1)} all-to-all(f32[4,256,256]{2,1,0:T(8,128)} %bitcast.60), channel_id=1, replica_groups=mesh['x'=4,'z'=8,'c'=2,'y'=4] {'x'}, dimensions={0} | all-to-all | bytes 2097152 | tf_op jit(solution)/shard_map/raw_basis/all_to_all | solution.py:14
  39.8 15.6 %all_to_all.69 = f32[8,32,256]{2,1,0:T(8,128)S(1)} all-to-all(f32[8,32,256]{2,1,0:T(8,128)S(1)} %bitcast.66), channel_id=1, replica_groups=mesh['x'=4,'z'=8,'c'=2,'y'=4] {'z'}, dimensions={0} | all-to-all | bytes 524288 | tf_op jit(solution)/shard_map/raw_basis/all_to_all | solution.py:14
  55.5 11.0 %all_to_all.70 = bf16[8,32,256]{2,1,0:T(8,128)(2,1)S(1)} all-to-all(bf16[8,32,256]{2,1,0:T(8,128)(2,1)S(1)} %broadcast_in_dim.13), channel_id=1, replica_groups=mesh['x'=4,'z'=8,'c'=2,'y'=4] {'z'}, dimensions={0} | all-to-all | bytes 262144 | tf_op jit(solution)/shard_map/raw_basis/all_to_all | solution.py:21
  66.5 10.9 %all_to_all.71 = bf16[4,256,256]{2,1,0:T(8,128)(2,1)S(1)} all-to-all(bf16[4,256,256]{2,1,0:T(8,128)(2,1)S(1)} %broadcast_in_dim.15), channel_id=1, replica_groups=mesh['x'=4,'z'=8,'c'=2,'y'=4] {'x'}, dimensions={0} | all-to-all | bytes 1048576 | tf_op jit(solution)/shard_map/raw_basis/all_to_all | solution.py:21
  77.4 10.8 %all_to_all.72 = bf16[2,1024,256]{2,1,0:T(8,128)(2,1)S(1)} all-to-all(bf16[2,1024,256]{2,1,0:T(8,128)(2,1)S(1)} %broadcast_in_dim.34), channel_id=1, replica_groups=mesh['x'=4,'z'=8,'c'=2,'y'=4] {'c'}, dimensions={0} | all-to-all | bytes 2097152 | tf_op jit(solution)/shard_map/raw_basis/all_to_all | solution.py:21
  88.3 1.3 fusion.22
  90.7 3.9 %all-to-all-start.6 = ((f32[4,256,256]{1,2,0:T(8,128)}), f32[4,256,256]{1,2,0:T(8,128)S(1)}, u32[]{:S(2)}, u32[]{:S(2)}) async-start(f32[4,256,256]{1,2,0:T(8,128)} %bitcast.53), calls=%async_computation.6 | async-start | bytes 2097152 | tf_op jit(solution)/shard_map/coords/all_to_all | solution.py:14
  94.7 14.4 %all-to-all-done.6 = f32[4,256,256]{1,2,0:T(8,128)S(1)} async-done(((f32[4,256,256]{1,2,0:T(8,128)}), f32[4,256,256]{1,2,0:T(8,128)S(1)}, u32[]{:S(2)}, u32[]{:S(2)}) %all-to-all-start.6) | async-done | bytes 1048608 | tf_op jit(solution)/shard_map/coords/all_to_all | solution.py:14
  110.0 24.0 %all_to_all.73 = f32[256,2,128]{2,1,0:T(2,128)S(1)} all-to-all(f32[256,2,128]{2,1,0:T(2,128)S(1)} %copy.14), channel_id=1, replica_groups=mesh['x'=4,'z'=8,'c'=2,'y'=4] {'x','z','c','y'}, dimensions={0} | all-to-all | bytes 524288 | tf_op jit(solution)/shard_map/curvature/all_to_all | solution.py:56
  135.1 5.7 %all-to-all-start.8 = ((f32[256,2,128]{2,1,0:T(2,128)}), f32[256,2,128]{2,1,0:T(2,128)S(1)}, u32[]{:S(2)}, u32[]{:S(2)}) async-start(f32[256,2,128]{2,1,0:T(2,128)} %broadcast_in_dim.35), calls=%async_computation.8 | async-start | bytes 524288 | tf_op jit(solution)/shard_map/curvature/all_to_all | solution.py:59
  141.0 15.6 %all-to-all-done.8 = f32[256,2,128]{2,1,0:T(2,128)S(1)} async-done(((f32[256,2,128]{2,1,0:T(2,128)}), f32[256,2,128]{2,1,0:T(2,128)S(1)}, u32[]{:S(2)}, u32[]{:S(2)}) %all-to-all-start.8) | async-done | bytes 262176 | tf_op jit(solution)/shard_map/curvature/all_to_all | solution.py:59
  156.9 11.7 %cholesky.50 = f32[128,128]{1,0:T(8,128)S(1)} custom-call(f32[128,128]{1,0:T(8,128)S(1)} %cholesky.118), custom_call_target="Cholesky" | custom-call | tf_op jit(solution)/shard_map/solve/jit(cholesky)/cholesky | solution.py:61
  168.7 9.8 %custom-call.18 = f32[1,128,128]{1,2,0:T(8,128)S(1)} custom-call(f32[1,128,128]{2,1,0:T(8,128)S(1)} %get-tuple-element.26), custom_call_target="InvertDiagBlocksLowerTriangular" | custom-call | tf_op jit(solution)/shard_map/solve/jit(cholesky)/cholesky | solution.py:61
  179.0 11.7 %cholesky.105 = f32[128,128]{1,0:T(8,128)S(1)} custom-call(f32[128,128]{1,0:T(8,128)S(1)} %convolution_subtract_fusion.2), custom_call_target="Cholesky" | custom-call | tf_op jit(solution)/shard_map/solve/jit(cholesky)/cholesky | solution.py:61
  192.8 4.1 %while.1 = (s32[]{:T(128)}, f32[256,256]{1,0:T(8,128)S(1)}, s32[2,2]{1,0:T(2,128)S(1)}, f32[2,128,128]{2,1,0:T(8,128)S(1)}, s32[]{:T(128)}) while((s32[]{:T(128)}, f32[256,256]{1,0:T(8,128)S(1)}, s32[2,2]{1,0:T(2,128)S(1)}, f32[2,128,128]{2,1,0:T(8,128)S(1)}, s32[]{:T(128)}) %tuple.24), condition=%wide.while_cond, body=%wide.while_body.sunk | while | flops 2 | bytes 131189 | solution.py:62
  193.6 1.3 bitcast_dynamic-update-slice_fusion.2
  195.5 1.3 bitcast_dynamic-update-slice_fusion.2
  196.9 19.7 %custom-call.19 = f32[2,128,128]{1,2,0:T(8,128)S(1)} custom-call(f32[2,128,128]{2,1,0:T(8,128)S(1)} %get-tuple-element.12), custom_call_target="InvertDiagBlocksLowerTriangular" | custom-call | tf_op jit(solution)/shard_map/solve/jit(_cho_solve)/triangular_solve | solution.py:62
  216.9 4.5 %convolution_bitcast_fusion = f32[1024,256]{0,1:T(8,128)} fusion(bf16[2048,256]{1,0:T(8,128)(2,1)S(1)} %bitcast.68, bf16[1024,2048]{1,0:T(8,128)(2,1)} %all-gather.2.cloned.1.call-done), kind=kOutput, calls=%fused_computation.2 | convolution fusion | flops 1073741824 | bytes 6291456 | tf_op jit(solution)/shard_map/coords/dot_general | solution.py:44
  222.8 41.5 %all-reduce.3.cloned.1.call-done = f32[1024,256]{0,1:T(8,128)} async-done(((f32[1024,256]{0,1:T(8,128)}), f32[1024,256]{0,1:T(8,128)}) %all-reduce.3.cloned.1.call-update) | async-done | bytes 1048592 | tf_op jit(solution)/shard_map/coords/psum | solution.py:45
  264.3 4.0 %convolution_multiply_fusion = f32[1024,256]{1,0:T(8,128)} fusion(f32[1024,256]{0,1:T(8,128)} %all-reduce.3.cloned.1.call-done, f32[128,256]{1,0:T(8,128)S(1)} %fusion.14, f32[128,256]{1,0:T(8,128)S(1)} %fusion.13), kind=kOutput, calls=%fused_computation.3 | convolution fusion | flops 805634048 | bytes 2359296 | tf_op jit(solution)/shard_map/dot_general | solution.py:63
  (47 shorter events, 9.1 us)
Async XLA Ops:
  6.5 1.0 copy-start
  6.5 210.4 %all-gather.2.cloned.1.call-start = ((), (), s32[]{:S(2)}) async-start(), calls=%async_computation.9 | async-start | bytes 4259840 | tf_op jit(solution)/shard_map/val_gather/all_gather | solution.py:32
  55.4 32.9 %copy-start.1 = (bf16[1024,2048]{1,0:T(8,128)(2,1)S(1)}, bf16[1024,2048]{1,0:T(8,128)(2,1)}, u32[]{:S(2)}) copy-start(bf16[1024,2048]{1,0:T(8,128)(2,1)} %param.3) | copy-start | bytes 12582916
  90.7 18.4 %all-to-all-start.6 = ((f32[4,256,256]{1,2,0:T(8,128)}), f32[4,256,256]{1,2,0:T(8,128)S(1)}, u32[]{:S(2)}, u32[]{:S(2)}) async-start(f32[4,256,256]{1,2,0:T(8,128)} %bitcast.53), calls=%async_computation.6 | async-start | bytes 2097152 | tf_op jit(solution)/shard_map/coords/all_to_all | solution.py:14
  135.1 21.5 %all-to-all-start.8 = ((f32[256,2,128]{2,1,0:T(2,128)}), f32[256,2,128]{2,1,0:T(2,128)S(1)}, u32[]{:S(2)}, u32[]{:S(2)}) async-start(f32[256,2,128]{2,1,0:T(2,128)} %broadcast_in_dim.35), calls=%async_computation.8 | async-start | bytes 524288 | tf_op jit(solution)/shard_map/curvature/all_to_all | solution.py:59
  140.8 123.6 %all-reduce.3.cloned.1.call-start = ((), (), s32[]{:S(2)}) async-start(), calls=%async_computation.10 | async-start | bytes 2097152 | tf_op jit(solution)/shard_map/coords/psum | solution.py:45
Sparse Core Ops, SparseCore 0:
  10.1 84.5 all-gather.1
  221.5 42.7 all-reduce.2

commit v2 on v1

v2 whole, which is shorter than its diff:
```python
import functools
import math

import jax
import jax.numpy as jnp
from jax import lax
from jax.experimental import pallas as pl
from jax.experimental.pallas import tpu as pltpu
from jax.sharding import Mesh, PartitionSpec as P

damping = 0.1
f32 = jnp.float32
highest = lax.Precision.HIGHEST
PIVOTS = 4
BAND = 64


def inverse_of_four(k):
    a, b, c = k[0][0], k[0][1], k[1][1]
    ra = 1.0 / (a * c - b * b)
    p, q, r = c * ra, -b * ra, a * ra
    e, f, g, h = k[0][2], k[0][3], k[1][2], k[1][3]
    y00, y01 = p * e + q * g, p * f + q * h
    y10, y11 = q * e + r * g, q * f + r * h
    s00 = k[2][2] - (e * y00 + g * y10)
    s01 = k[2][3] - (e * y01 + g * y11)
    s11 = k[3][3] - (f * y01 + h * y11)
    rs = 1.0 / (s00 * s11 - s01 * s01)
    u, v, w = s11 * rs, -s01 * rs, s00 * rs
    z00, z01 = y00 * u + y01 * v, y00 * v + y01 * w
    z10, z11 = y10 * u + y11 * v, y10 * v + y11 * w
    i00 = p + z00 * y00 + z01 * y01
    i01 = q + z00 * y10 + z01 * y11
    i11 = r + z10 * y10 + z11 * y11
    return [
        [i00, i01, -z00, -z01],
        [i01, i11, -z10, -z11],
        [-z00, -z10, u, v],
        [-z01, -z11, v, w],
    ]


def solve_body(m_ref, x_ref, o_ref, e_ref, *, scale):
    n = m_ref.shape[0]
    rows = lax.broadcasted_iota(jnp.int32, (n, n), 0)
    cols = lax.broadcasted_iota(jnp.int32, (n, n), 1)
    m = m_ref[...]
    diagonal = jnp.where(rows == cols, m, 0.0)
    along = lax.rsqrt(jnp.sum(diagonal, axis=0, keepdims=True))
    down = lax.rsqrt(jnp.sum(diagonal, axis=1, keepdims=True))
    e_ref[:, :n] = m * along * down
    e_ref[:, n:] = x_ref[...].T * down
    tiles = BAND // 8
    chunks = 2 * n // 128
    sub = lax.broadcasted_iota(jnp.int32, (8, 128), 0)
    band_row = lax.broadcasted_iota(jnp.int32, (n, BAND), 0)
    for lo in range(0, n, BAND):
        first = lo // 128
        panel = {
            c: e_ref[lo : lo + BAND, c * 128 : (c + 1) * 128].reshape(tiles, 8, 128)
            for c in range(first, chunks)
        }
        for g in range(0, BAND, PIVOTS):
            tile, s = g // 8, g % 8
            d, lane = (lo + g) // 128, (lo + g) % 128
            column = [
                jnp.broadcast_to(panel[d][:, :, lane + a : lane + a + 1], (tiles, 8, 128))
                for a in range(PIVOTS)
            ]
            block = [
                [
                    jnp.broadcast_to(column[b][tile, s + a : s + a + 1, :], (8, 128))
                    for b in range(PIVOTS)
                ]
                for a in range(PIVOTS)
            ]
            inv = inverse_of_four(block)
            for c in range(d, chunks):
                old = [
                    jnp.broadcast_to(panel[c][tile, s + a : s + a + 1, :], (8, 128))
                    for a in range(PIVOTS)
                ]
                new = [sum(inv[a][b] * old[b] for b in range(PIVOTS)) for a in range(PIVOTS)]
                out = []
                for t in range(tiles):
                    value = panel[c][t] - sum(column[a][t] * new[a] for a in range(PIVOTS))
                    if t == tile:
                        for a in range(PIVOTS):
                            value = jnp.where(sub == s + a, new[a], value)
                    out.append(value)
                panel[c] = jnp.stack(out, axis=0)
        wide = jnp.concatenate(
            [panel[c].reshape(BAND, 128) for c in range(first, chunks)], axis=1
        )
        left = e_ref[:, lo : lo + BAND]
        left = jnp.where((band_row >= lo) & (band_row < lo + BAND), 0.0, left)
        e_ref[:, first * 128 :] = e_ref[:, first * 128 :] - jnp.dot(
            left, wide, precision=highest, preferred_element_type=f32
        )
        e_ref[lo : lo + BAND, first * 128 :] = wide
    o_ref[...] = e_ref[:, n:] * (down * scale)


def solve(m, x, scale):
    n = m.shape[0]
    return pl.pallas_call(
        functools.partial(solve_body, scale=scale),
        out_shape=jax.ShapeDtypeStruct((n, n), f32),
        in_specs=[pl.BlockSpec(memory_space=pltpu.VMEM)] * 2,
        out_specs=pl.BlockSpec(memory_space=pltpu.VMEM),
        scratch_shapes=[pltpu.VMEM((n, 2 * n), f32)],
        compiler_params=pltpu.CompilerParams(vmem_limit_bytes=16 * 2**20),
        cost_estimate=pl.CostEstimate(
            flops=4 * n**3, bytes_accessed=12 * n * n, transcendentals=n * n
        ),
        name="solve",
    )(m, x)


def members(sizes, axes):
    return math.prod(sizes[a] for a in axes)


def scatter_sum(sizes, value, axes):
    n = members(sizes, axes)
    parts = lax.all_to_all(value, axes, 0, 0, tiled=True)
    return jnp.sum(parts.reshape((n, value.shape[0] // n) + value.shape[1:]), axis=0)


def gather(sizes, value, axes):
    n = members(sizes, axes)
    copies = jnp.broadcast_to(value[None], (n,) + value.shape)
    rows = copies.reshape((n * value.shape[0],) + value.shape[1:])
    return lax.all_to_all(rows, axes, 0, 0, tiled=True)


def local(sizes, training_grads, validation_grads, test_matrix):
    row_count = training_grads.shape[0]
    val_rows = validation_grads.shape[0]
    rank_size = test_matrix.shape[1]
    total_train = row_count * members(sizes, ("x", "z", "c"))
    planes = members(sizes, ("x", "z"))
    with jax.named_scope("val_gather"):
        val_block = lax.all_gather(validation_grads, ("x", "z"), axis=0, tiled=True)
    with jax.named_scope("raw_basis"):
        basis_rows = lax.dot_general(
            training_grads, test_matrix, (((0,), (0,)), ((), ())), preferred_element_type=f32
        )
        for axis in ("c", "x", "z"):
            basis_rows = scatter_sum(sizes, basis_rows, (axis,))
        basis = basis_rows.astype(jnp.bfloat16)
        basis = gather(sizes, basis, ("x", "z"))
        basis = gather(sizes, basis, ("c",))
    with jax.named_scope("coords"):
        val_part = jnp.dot(val_block, basis, preferred_element_type=f32)
        train_part = jnp.dot(training_grads, basis, preferred_element_type=f32)
        train_part, val_part = lax.optimization_barrier((train_part, val_part))
        val_half = lax.psum(val_part, "y")
        mine = scatter_sum(sizes, train_part, ("y",))
    with jax.named_scope("curvature"):
        first = (((0,), (0,)), ((), ()))
        part = lax.dot_general(mine, mine, first, precision=highest) / total_train
        part = part + damping * lax.dot_general(basis_rows, basis_rows, first, precision=highest)
        part = scatter_sum(sizes, part, ("z", "c"))
        part = jnp.sum(gather(sizes, part, ("x", "y")).reshape((-1,) + part.shape), axis=0)
        curvature = gather(sizes, part, ("z", "c"))
    with jax.named_scope("solve"):
        solved = solve(curvature, mine, 1.0 / math.sqrt(rank_size))
    with jax.named_scope("scores"):
        swap = [(0, 1), (1, 0)]
        other = lax.ppermute(val_half, "c", swap)
        even = lax.axis_index("c") == 0
        halves = [jnp.where(even, val_half, other), jnp.where(even, other, val_half)]
        halves = [h.reshape(planes, val_rows, rank_size) for h in halves]
        val_coords = jnp.stack(halves, axis=1).reshape(planes * 2 * val_rows, rank_size)
        return jnp.dot(val_coords, solved, precision=lax.Precision.HIGH)


def solution(mesh):
    sizes = {"x": 4, "z": 8, "c": 2, "y": 4}
    split = Mesh(mesh.devices.reshape(tuple(sizes.values())), tuple(sizes))
    dp = ("x", "z", "c")

    def run(training_grads, validation_grads, test_matrix):
        return jax.shard_map(
            functools.partial(local, sizes),
            mesh=split,
            in_specs=(P(dp, "y"), P(dp, "y"), P(dp, None)),
            out_specs=P(None, dp + ("y",)),
            check_vma=False,
        )(training_grads, validation_grads, test_matrix)

    return run
```

time: 276 us -> 213 us (0.77)
  other arithmetic: 55.4 us -> 2.63 us
  waiting for transfers between devices: 72.2 us -> 55.1 us
  starting transfers between devices: 9.82 us -> 25.9 us
  Pallas kernels: 0 us -> 15.9 us
  blocking collectives: 99.7 us -> 85.8 us
  matrix products: 16.1 us -> 11.1 us
  local copies, waits for them, and re-layouts: 6.74 us -> 2.87 us
    another operation x9 -> x1, other arithmetic: 53.7 us -> 0.07 us  [local(): jnp.stack(halves, axis=1).reshape(planes * 2 * val_rows, rank_size)]
    pallas_call x0 -> x1, Pallas kernels: none -> 15.9 us  [solve(): pl.pallas_call(functools.partial(solve_body, scale=scale), out_shape=jax....]
    all_to_all x7 -> x6, blocking collectives: 99.7 us -> 85.8 us  [the longest x3 42.9 us: scatter_sum(): parts = lax.all_to_all(value, axes, 0, 0, tiled=True)]
    all_to_all x2 -> x3, starting transfers between devices: 9.6 us -> 23.4 us  [the longest x2 14.7 us: scatter_sum(): parts = lax.all_to_all(value, axes, 0, 0, tiled=True)]
    psum x1, waiting for transfers between devices: 41.5 us -> 29.8 us  [local(): val_half = lax.psum(val_part, 'y')]
    all_to_all x2 -> x3, waiting for transfers between devices: 30 us -> 19.9 us  [the longest x2 10 us: scatter_sum(): parts = lax.all_to_all(value, axes, 0, 0, tiled=True)]
    all_gather x1, waiting for transfers between devices: 0.02 us -> 4.45 us  [local(): val_block = lax.all_gather(validation_grads, ('x', 'z'), axis=0, tiled=True)]
    another operation x9 -> x1, local copies, waits for them, and re-layouts: 3.97 us -> 0.09 us  [local(): jnp.stack(halves, axis=1).reshape(planes * 2 * val_rows, rank_size)]
  transfers between devices with their start and end apart: 4 -> 6, of which waited for: 3 -> 4; matrix products, arithmetic and copies ran while one was open for 25% -> 5% of each run, Pallas kernels for 0% -> 0%
where the time goes in v2:
time: 213 us
  blocking collectives  85.8 us (40%)
  waiting for transfers between devices  55.1 us (26%)
  starting transfers between devices  25.9 us (12%)
  Pallas kernels  15.9 us (7%)
  between operations  13.5 us (6%)
  matrix products  11.1 us (5%)
  local copies, waits for them, and re-layouts  2.87 us (1%)
  other arithmetic  2.63 us (1%)
    all_to_all x3, blocking collectives, scatter_sum(): parts = lax.all_to_all(value, axes, 0, 0, tiled=True)  42.9 us
    all_to_all x3, blocking collectives, gather(): return lax.all_to_all(rows, axes, 0, 0, tiled=True)  42.9 us
    psum x1, waiting for transfers between devices, local(): val_half = lax.psum(val_part, 'y')  29.8 us
    pallas_call x1, Pallas kernels, solve(): pl.pallas_call(functools.partial(solve_body, scale=scale), out_shape=jax....  15.9 us
    all_to_all x2, starting transfers between devices, scatter_sum(): parts = lax.all_to_all(value, axes, 0, 0, tiled=True)  14.7 us
    all_to_all x2, waiting for transfers between devices, scatter_sum(): parts = lax.all_to_all(value, axes, 0, 0, tiled=True)  10 us
    all_to_all x1, waiting for transfers between devices, gather(): return lax.all_to_all(rows, axes, 0, 0, tiled=True)  9.83 us
    all_to_all x1, starting transfers between devices, gather(): return lax.all_to_all(rows, axes, 0, 0, tiled=True)  8.65 us
  transfers between devices with their start and end apart: 6, of which 4 were waited for; matrix products, arithmetic and copies ran while one was open for 5% of the time, Pallas kernels for 0%

profile of v2, /device:TPU:1, one launch (start us, length us, event | category | flops | bytes accessed | tf_op | source)
XLA Modules:
  0.0 212.8 jit_solution(11658651130079479943)
XLA Ops:
  7.6 3.5 %fusion.1 = f32[2048,256]{1,0:T(8,128)S(1)} fusion(bf16[1024,2048]{1,0:T(8,128)(2,1)} %param.3, bf16[1024,256]{1,0:T(8,128)(2,1)S(1)} %copy-done), kind=kOutput, calls=%fused_computation.9 | convolution fusion | flops 1073741824 | bytes 6815744 | tf_op jit(solution)/shard_map/raw_basis/dot_general | solution.py:146
  11.1 8.3 %all_to_all.74 = f32[2,1024,256]{2,1,0:T(8,128)S(1)} all-to-all(f32[2,1024,256]{2,1,0:T(8,128)S(1)} %bitcast.34), channel_id=1, replica_groups=mesh['x'=4,'z'=8,'c'=2,'y'=4] {'c'}, dimensions={0} | all-to-all | bytes 4194304 | tf_op jit(solution)/shard_map/raw_basis/all_to_all | solution.py:126
  19.4 1.2 reduce_sum.54
  20.6 19.1 %all_to_all.75 = f32[4,256,256]{2,1,0:T(8,128)S(1)} all-to-all(f32[4,256,256]{2,1,0:T(8,128)} %bitcast.32), channel_id=1, replica_groups=mesh['x'=4,'z'=8,'c'=2,'y'=4] {'x'}, dimensions={0} | all-to-all | bytes 2097152 | tf_op jit(solution)/shard_map/raw_basis/all_to_all | solution.py:126
  39.8 15.5 %all_to_all.76 = f32[8,32,256]{2,1,0:T(8,128)S(1)} all-to-all(f32[8,32,256]{2,1,0:T(8,128)S(1)} %bitcast.37), channel_id=1, replica_groups=mesh['x'=4,'z'=8,'c'=2,'y'=4] {'z'}, dimensions={0} | all-to-all | bytes 524288 | tf_op jit(solution)/shard_map/raw_basis/all_to_all | solution.py:126
  55.4 17.0 %all_to_all.77 = bf16[32,32,256]{2,1,0:T(8,128)(2,1)S(1)} all-to-all(bf16[32,32,256]{2,1,0:T(8,128)(2,1)S(1)} %broadcast_in_dim.10), channel_id=1, replica_groups=mesh['x'=4,'z'=8,'c'=2,'y'=4] {'x','z'}, dimensions={0} | all-to-all | bytes 1048576 | tf_op jit(solution)/shard_map/raw_basis/all_to_all | solution.py:134
  72.4 12.4 %all_to_all.78 = bf16[2,1024,256]{2,1,0:T(8,128)(2,1)S(1)} all-to-all(bf16[2,1024,256]{2,1,0:T(8,128)(2,1)S(1)} %broadcast_in_dim.12), channel_id=1, replica_groups=mesh['x'=4,'z'=8,'c'=2,'y'=4] {'c'}, dimensions={0} | all-to-all | bytes 2097152 | tf_op jit(solution)/shard_map/raw_basis/all_to_all | solution.py:134
  84.9 1.3 convolution_bitcast_fusion
  86.2 4.4 %all-gather.2.cloned.1.call-done = bf16[512,2048]{1,0:T(8,128)(2,1)} async-done(((bf16[16,2048]{1,0:T(8,128)(2,1)}), bf16[512,2048]{1,0:T(8,128)(2,1)}) %all-gather.2.cloned.1.call-update) | async-done | bytes 2097168 | tf_op jit(solution)/shard_map/val_gather/all_gather | solution.py:144
  90.6 3.1 %convolution_bitcast_fusion.1 = f32[512,256]{0,1:T(8,128)} fusion(bf16[2048,256]{1,0:T(8,128)(2,1)S(1)} %bitcast.40, bf16[512,2048]{1,0:T(8,128)(2,1)} %all-gather.2.cloned.1.call-done), kind=kOutput, calls=%fused_computation.1 | convolution fusion | flops 536870912 | bytes 3670016 | tf_op jit(solution)/shard_map/coords/dot_general | solution.py:155
  93.8 1.1 copy.22
  94.8 4.8 %all-to-all-start.5 = ((f32[4,256,256]{1,2,0:T(8,128)}), f32[4,256,256]{1,2,0:T(8,128)S(1)}, u32[]{:S(2)}, u32[]{:S(2)}) async-start(f32[4,256,256]{1,2,0:T(8,128)} %bitcast.29), calls=%async_computation.5 | async-start | bytes 2097152 | tf_op jit(solution)/shard_map/coords/all_to_all | solution.py:126
  100.3 10.0 %all-to-all-done.5 = f32[4,256,256]{1,2,0:T(8,128)S(1)} async-done(((f32[4,256,256]{1,2,0:T(8,128)}), f32[4,256,256]{1,2,0:T(8,128)S(1)}, u32[]{:S(2)}, u32[]{:S(2)}) %all-to-all-start.5) | async-done | bytes 1048608 | tf_op jit(solution)/shard_map/coords/all_to_all | solution.py:126
  110.5 1.1 fusion
  111.6 10.0 %all-to-all-start.6 = ((f32[16,16,256]{2,1,0:T(8,128)}), f32[16,16,256]{2,1,0:T(8,128)S(1)}, u32[]{:S(2)}, u32[]{:S(2)}) async-start(f32[16,16,256]{2,1,0:T(8,128)} %bitcast.10), calls=%async_computation.6 | async-start | bytes 524288 | tf_op jit(solution)/shard_map/curvature/all_to_all | solution.py:126
  121.5 29.8 %all-reduce.2.cloned.1.call-done = f32[512,256]{0,1:T(8,128)} async-done(((f32[512,256]{0,1:T(8,128)}), f32[512,256]{0,1:T(8,128)}) %all-reduce.2.cloned.1.call-update) | async-done | bytes 524304 | tf_op jit(solution)/shard_map/coords/psum | solution.py:158
  151.3 2.5 %collective-permute-start = (f32[512,256]{0,1:T(8,128)}, f32[512,256]{0,1:T(8,128)S(1)}, u32[]{:S(2)}, u32[]{:S(2)}) collective-permute-start(f32[512,256]{0,1:T(8,128)} %all-reduce.2.cloned.1.call-done), channel_id=1, source_target_pairs={{0,4},{4,0},{1,5},{5,1},{2,6},{6,2},{3,7},{7,3},{8,12},{12,8},{9,1... | collective-permute-start | bytes 1572872 | tf_op jit(solution)/shard_map/scores/ppermute | solution.py:171
  153.8 13.5 %all_to_all.79 = f32[16,16,256]{2,1,0:T(8,128)S(1)} all-to-all(f32[16,16,256]{2,1,0:T(8,128)S(1)} %broadcast_in_dim.13), channel_id=1, replica_groups=mesh['x'=4,'z'=8,'c'=2,'y'=4] {'x','y'}, dimensions={0} | all-to-all | bytes 524288 | tf_op jit(solution)/shard_map/curvature/all_to_all | solution.py:134
  167.4 0.7 broadcast_in_dim.14
  168.1 8.7 %all-to-all-start.8 = ((f32[16,16,256]{2,1,0:T(8,128)}), f32[16,16,256]{2,1,0:T(8,128)S(1)}, u32[]{:S(2)}, u32[]{:S(2)}) async-start(f32[16,16,256]{2,1,0:T(8,128)} %broadcast_in_dim.14), calls=%async_computation.8 | async-start | bytes 524288 | tf_op jit(solution)/shard_map/curvature/all_to_all | solution.py:134
  176.9 1.1 broadcast_select_fusion.1
  178.6 9.8 %all-to-all-done.8 = f32[16,16,256]{2,1,0:T(8,128)S(1)} async-done(((f32[16,16,256]{2,1,0:T(8,128)}), f32[16,16,256]{2,1,0:T(8,128)S(1)}, u32[]{:S(2)}, u32[]{:S(2)}) %all-to-all-start.8) | async-done | bytes 262176 | tf_op jit(solution)/shard_map/curvature/all_to_all | solution.py:134
  188.4 15.9 %solve.1 = f32[256,256]{1,0:T(8,128)S(1)} custom-call(f32[256,256]{1,0:T(8,128)S(1)} %bitcast.30, f32[256,256]{1,0:T(8,128)S(1)} %copy.18.x_ref), custom_call_target="tpu_custom_call" | custom-call | flops 67108864 | bytes 786432 | tf_op jit(solution)/shard_map/solve/solve/pallas_call | solution.py:106
  204.4 1.6 fusion.2
  (25 shorter events, 2.8 us)
Async XLA Ops:
  6.5 1.0 copy-start
  6.5 84.1 %all-gather.2.cloned.1.call-start = ((), (), s32[]{:S(2)}) async-start(), calls=%async_computation.9 | async-start | bytes 2162688 | tf_op jit(solution)/shard_map/val_gather/all_gather | solution.py:144
  55.3 29.5 %copy-start.1 = (bf16[1024,2048]{1,0:T(8,128)(2,1)S(1)}, bf16[1024,2048]{1,0:T(8,128)(2,1)}, u32[]{:S(2)}) copy-start(bf16[1024,2048]{1,0:T(8,128)(2,1)} %param.3) | copy-start | bytes 12582916
  94.8 15.5 %all-to-all-start.5 = ((f32[4,256,256]{1,2,0:T(8,128)}), f32[4,256,256]{1,2,0:T(8,128)S(1)}, u32[]{:S(2)}, u32[]{:S(2)}) async-start(f32[4,256,256]{1,2,0:T(8,128)} %bitcast.29), calls=%async_computation.5 | async-start | bytes 2097152 | tf_op jit(solution)/shard_map/coords/all_to_all | solution.py:126
  99.6 51.7 %all-reduce.2.cloned.1.call-start = ((), (), s32[]{:S(2)}) async-start(), calls=%async_computation.10 | async-start | bytes 1048576 | tf_op jit(solution)/shard_map/coords/psum | solution.py:158
  111.6 42.2 %all-to-all-start.6 = ((f32[16,16,256]{2,1,0:T(8,128)}), f32[16,16,256]{2,1,0:T(8,128)S(1)}, u32[]{:S(2)}, u32[]{:S(2)}) async-start(f32[16,16,256]{2,1,0:T(8,128)} %bitcast.10), calls=%async_computation.6 | async-start | bytes 524288 | tf_op jit(solution)/shard_map/curvature/all_to_all | solution.py:126
  151.3 25.6 %collective-permute-start = (f32[512,256]{0,1:T(8,128)}, f32[512,256]{0,1:T(8,128)S(1)}, u32[]{:S(2)}, u32[]{:S(2)}) collective-permute-start(f32[512,256]{0,1:T(8,128)} %all-reduce.2.cloned.1.call-done), channel_id=1, source_target_pairs={{0,4},{4,0},{1,5},{5,1},{2,6},{6,2},{3,7},{7,3},{8,12},{12,8},{9,1... | collective-permute-start | bytes 1572872 | tf_op jit(solution)/shard_map/scores/ppermute | solution.py:171
  168.1 20.4 %all-to-all-start.8 = ((f32[16,16,256]{2,1,0:T(8,128)}), f32[16,16,256]{2,1,0:T(8,128)S(1)}, u32[]{:S(2)}, u32[]{:S(2)}) async-start(f32[16,16,256]{2,1,0:T(8,128)} %broadcast_in_dim.14), calls=%async_computation.8 | async-start | bytes 524288 | tf_op jit(solution)/shard_map/curvature/all_to_all | solution.py:134
Sparse Core Ops, SparseCore 0:
  10.0 80.6 all-gather.1
  102.8 48.4 all-reduce.1

commit v3 on v2

--- a/solution.py
+++ b/solution.py
@@ -140,8 +140,9 @@
     rank_size = test_matrix.shape[1]
     total_train = row_count * members(sizes, ("x", "z", "c"))
     planes = members(sizes, ("x", "z"))
-    with jax.named_scope("val_gather"):
-        val_block = lax.all_gather(validation_grads, ("x", "z"), axis=0, tiled=True)
+    feats = sizes["y"]
+    quarter = row_count // feats
+    val_share = val_rows // feats
     with jax.named_scope("raw_basis"):
         basis_rows = lax.dot_general(
             training_grads, test_matrix, (((0,), (0,)), ((), ())), preferred_element_type=f32
@@ -152,27 +153,56 @@
         basis = gather(sizes, basis, ("x", "z"))
         basis = gather(sizes, basis, ("c",))
     with jax.named_scope("coords"):
-        val_part = jnp.dot(val_block, basis, preferred_element_type=f32)
         train_part = jnp.dot(training_grads, basis, preferred_element_type=f32)
-        train_part, val_part = lax.optimization_barrier((train_part, val_part))
-        val_half = lax.psum(val_part, "y")
-        mine = scatter_sum(sizes, train_part, ("y",))
+        val_part = jnp.dot(validation_grads, basis, preferred_element_type=f32)
+        both = jnp.concatenate(
+            [
+                train_part.reshape(feats, quarter, rank_size),
+                val_part.reshape(feats, val_share, rank_size),
+                jnp.zeros((feats, 8 - val_share, rank_size), f32),
+            ],
+            axis=1,
+        )
+        both = jnp.sum(lax.all_to_all(both, "y", 0, 0, tiled=True), axis=0)
+        mine, val_mine = both[:quarter], both[quarter : quarter + val_share]
     with jax.named_scope("curvature"):
         first = (((0,), (0,)), ((), ()))
         part = lax.dot_general(mine, mine, first, precision=highest) / total_train
         part = part + damping * lax.dot_general(basis_rows, basis_rows, first, precision=highest)
-        part = scatter_sum(sizes, part, ("z", "c"))
-        part = jnp.sum(gather(sizes, part, ("x", "y")).reshape((-1,) + part.shape), axis=0)
+        zc = members(sizes, ("z", "c"))
+        xy = members(sizes, ("x", "y"))
+        share = rank_size // zc
+        halves = jnp.broadcast_to(
+            val_mine.reshape(1, 2, val_share // 2, rank_size),
+            (sizes["z"], 2, val_share // 2, rank_size),
+        ).reshape(zc, val_share // 2, rank_size)
+        send = jnp.concatenate(
+            [
+                part.reshape(zc, share, rank_size),
+                halves,
+                jnp.zeros((zc, 8 - val_share // 2, rank_size), f32),
+            ],
+            axis=1,
+        )
+        got = lax.all_to_all(send, ("z", "c"), 0, 0, tiled=True)
+        part = jnp.sum(got[:, :share], axis=0)
+        val_held = got[:, share : share + val_share // 2].reshape(zc * val_share // 2, rank_size)
+        send = jnp.concatenate([part, val_held], axis=0)
+        send = jnp.broadcast_to(send[None], (xy,) + send.shape)
+        got = lax.all_to_all(send, ("x", "y"), 0, 0, tiled=True)
+        part = jnp.sum(got[:, :share], axis=0)
+        val_half = got[:, share:].reshape(
+            sizes["x"], feats, sizes["z"], 2, 1, val_share // 2, rank_size
+        )
         curvature = gather(sizes, part, ("z", "c"))
     with jax.named_scope("solve"):
+        other = lax.ppermute(val_half, "c", [(0, 1), (1, 0)])
         solved = solve(curvature, mine, 1.0 / math.sqrt(rank_size))
     with jax.named_scope("scores"):
-        swap = [(0, 1), (1, 0)]
-        other = lax.ppermute(val_half, "c", swap)
         even = lax.axis_index("c") == 0
-        halves = [jnp.where(even, val_half, other), jnp.where(even, other, val_half)]
-        halves = [h.reshape(planes, val_rows, rank_size) for h in halves]
-        val_coords = jnp.stack(halves, axis=1).reshape(planes * 2 * val_rows, rank_size)
+        pair = [jnp.where(even, val_half, other), jnp.where(even, other, val_half)]
+        val_coords = jnp.concatenate(pair, axis=4).transpose(0, 2, 3, 1, 4, 5, 6)
+        val_coords = val_coords.reshape(planes * 2 * val_rows, rank_size)
         return jnp.dot(val_coords, solved, precision=lax.Precision.HIGH)
 
 

time: 213 us -> 177 us (0.83)
  waiting for transfers between devices: 55.1 us -> 37.5 us
  starting transfers between devices: 25.9 us -> 12.4 us
  between operations: 13.5 us -> 0.23 us
  blocking collectives: 85.8 us -> 89.8 us
  local copies, waits for them, and re-layouts: 2.87 us -> 6.26 us
    all_to_all x0 -> x2, blocking collectives: none -> 37.6 us  [the longest x1 20.4 us: local(): got = lax.all_to_all(send, ('z', 'c'), 0, 0, tiled=True)]
    all_to_all x3 -> x1, blocking collectives: 42.9 us -> 10.2 us  [gather(): return lax.all_to_all(rows, axes, 0, 0, tiled=True)]
    psum x1 -> x0, waiting for transfers between devices: 29.8 us -> none  [local(): val_half = lax.psum(val_part, 'y')]
    all_to_all x1 -> x2, waiting for transfers between devices: 9.83 us -> 23.1 us  [gather(): return lax.all_to_all(rows, axes, 0, 0, tiled=True)]
    all_to_all x2 -> x1, starting transfers between devices: 14.7 us -> 4.18 us  [local(): both = jnp.sum(lax.all_to_all(both, 'y', 0, 0, tiled=True), axis=0)]
    all_gather x1 -> x0, waiting for transfers between devices: 4.45 us -> none  [local(): val_block = lax.all_gather(validation_grads, ('x', 'z'), axis=0, tiled=True)]
    all_to_all x2 -> x1, waiting for transfers between devices: 10 us -> 14.4 us  [local(): both = jnp.sum(lax.all_to_all(both, 'y', 0, 0, tiled=True), axis=0)]
    dot_general x1, matrix products: 1.32 us -> 4.46 us  [local(): train_part = jnp.dot(training_grads, basis, preferred_element_type=f32)]
  transfers between devices with their start and end apart: 6 -> 4, of which waited for: 4 -> 3; matrix products, arithmetic and copies ran while one was open for 5% -> 1% of each run, Pallas kernels for 0% -> 9%
where the time goes in v3:
time: 177 us
  blocking collectives  89.8 us (51%)
  waiting for transfers between devices  37.5 us (21%)
  Pallas kernels  15.9 us (9%)
  starting transfers between devices  12.4 us (7%)
  matrix products  10.8 us (6%)
  local copies, waits for them, and re-layouts  6.26 us (4%)
  other arithmetic  3.8 us (2%)
    all_to_all x3, blocking collectives, scatter_sum(): parts = lax.all_to_all(value, axes, 0, 0, tiled=True)  42 us
    all_to_all x2, waiting for transfers between devices, gather(): return lax.all_to_all(rows, axes, 0, 0, tiled=True)  23.1 us
    all_to_all x1, blocking collectives, local(): got = lax.all_to_all(send, ('z', 'c'), 0, 0, tiled=True)  20.4 us
    all_to_all x1, blocking collectives, local(): got = lax.all_to_all(send, ('x', 'y'), 0, 0, tiled=True)  17.2 us
    pallas_call x1, Pallas kernels, solve(): pl.pallas_call(functools.partial(solve_body, scale=scale), out_shape=jax....  15.9 us
    all_to_all x1, waiting for transfers between devices, local(): both = jnp.sum(lax.all_to_all(both, 'y', 0, 0, tiled=True), axis=0)  14.4 us
    all_to_all x1, blocking collectives, gather(): return lax.all_to_all(rows, axes, 0, 0, tiled=True)  10.2 us
    all_to_all x2, starting transfers between devices, gather(): return lax.all_to_all(rows, axes, 0, 0, tiled=True)  7.5 us
  transfers between devices with their start and end apart: 4, of which 3 were waited for; matrix products, arithmetic and copies ran while one was open for 1% of the time, Pallas kernels for 9%

profile of v3, /device:TPU:1, one launch (start us, length us, event | category | flops | bytes accessed | tf_op | source)
XLA Modules:
  0.0 176.8 jit_solution(14343777722437834974)
XLA Ops:
  0.0 1.0 copy-done
  1.0 3.5 %fusion.2 = f32[2048,256]{1,0:T(8,128)S(1)} fusion(bf16[1024,2048]{1,0:T(8,128)(2,1)} %param.3, bf16[1024,256]{1,0:T(8,128)(2,1)S(1)} %copy-done), kind=kOutput, calls=%fused_computation.14 | convolution fusion | flops 1073741824 | bytes 6815744 | tf_op jit(solution)/shard_map/raw_basis/dot_general | solution.py:147
  4.6 8.3 %all_to_all.65 = f32[2,1024,256]{2,1,0:T(8,128)S(1)} all-to-all(f32[2,1024,256]{2,1,0:T(8,128)S(1)} %bitcast.31), channel_id=1, replica_groups=mesh['x'=4,'z'=8,'c'=2,'y'=4] {'c'}, dimensions={0} | all-to-all | bytes 4194304 | tf_op jit(solution)/shard_map/raw_basis/all_to_all | solution.py:126
  12.9 1.2 reduce_sum.54
  14.1 18.3 %all_to_all.66 = f32[4,256,256]{2,1,0:T(8,128)S(1)} all-to-all(f32[4,256,256]{2,1,0:T(8,128)} %bitcast.29), channel_id=1, replica_groups=mesh['x'=4,'z'=8,'c'=2,'y'=4] {'x'}, dimensions={0} | all-to-all | bytes 2097152 | tf_op jit(solution)/shard_map/raw_basis/all_to_all | solution.py:126
  32.5 15.4 %all_to_all.67 = f32[8,32,256]{2,1,0:T(8,128)S(1)} all-to-all(f32[8,32,256]{2,1,0:T(8,128)S(1)} %bitcast.33), channel_id=1, replica_groups=mesh['x'=4,'z'=8,'c'=2,'y'=4] {'z'}, dimensions={0} | all-to-all | bytes 524288 | tf_op jit(solution)/shard_map/raw_basis/all_to_all | solution.py:126
  47.9 0.9 broadcast_in_dim.18
  48.8 3.9 %all-to-all-start.3 = ((bf16[32,32,256]{2,1,0:T(8,128)(2,1)}), bf16[32,32,256]{2,1,0:T(8,128)(2,1)S(1)}, u32[]{:S(2)}, u32[]{:S(2)}) async-start(bf16[32,32,256]{2,1,0:T(8,128)(2,1)} %broadcast_in_dim.18), calls=%async_computation.3 | async-start | bytes 1048576 | tf_op jit(solution)/shard_map/raw_basis/all_to_all | solution.py:134
  52.7 11.6 %all-to-all-done.3 = bf16[32,32,256]{2,1,0:T(8,128)(2,1)S(1)} async-done(((bf16[32,32,256]{2,1,0:T(8,128)(2,1)}), bf16[32,32,256]{2,1,0:T(8,128)(2,1)S(1)}, u32[]{:S(2)}, u32[]{:S(2)}) %all-to-all-start.3) | async-done | bytes 524320 | tf_op jit(solution)/shard_map/raw_basis/all_to_all | solution.py:134
  64.4 10.2 %all_to_all.68 = bf16[2,1024,256]{2,1,0:T(8,128)(2,1)S(1)} all-to-all(bf16[2,1024,256]{2,1,0:T(8,128)(2,1)S(1)} %broadcast_in_dim.20), channel_id=1, replica_groups=mesh['x'=4,'z'=8,'c'=2,'y'=4] {'c'}, dimensions={0} | all-to-all | bytes 2097152 | tf_op jit(solution)/shard_map/raw_basis/all_to_all | solution.py:134
  74.6 4.5 %convolution_bitcast_fusion = f32[1024,256]{0,1:T(8,128)} fusion(bf16[2048,256]{1,0:T(8,128)(2,1)S(1)} %bitcast.27, bf16[1024,2048]{1,0:T(8,128)(2,1)} %param.3), kind=kOutput, calls=%fused_computation | convolution fusion | flops 1073741824 | bytes 6291456 | tf_op jit(solution)/shard_map/coords/dot_general | solution.py:156
  79.1 1.6 copy.23
  80.9 1.1 maximum_maximum_fusion
  82.1 4.2 %all-to-all-start.5 = ((f32[4,264,256]{2,1,0:T(8,128)}), f32[4,264,256]{2,1,0:T(8,128)S(1)}, u32[]{:S(2)}, u32[]{:S(2)}) async-start(f32[4,264,256]{2,1,0:T(8,128)} %maximum_maximum_fusion), calls=%async_computation.5 | async-start | bytes 2162688 | tf_op jit(solution)/shard_map/coords/all_to_all | solution.py:166
  86.7 14.4 %all-to-all-done.5 = f32[4,264,256]{2,1,0:T(8,128)S(1)} async-done(((f32[4,264,256]{2,1,0:T(8,128)}), f32[4,264,256]{2,1,0:T(8,128)S(1)}, u32[]{:S(2)}, u32[]{:S(2)}) %all-to-all-start.5) | async-done | bytes 1081376 | tf_op jit(solution)/shard_map/coords/all_to_all | solution.py:166
  102.0 20.4 %all_to_all.69 = f32[16,24,256]{2,1,0:T(8,128)S(1)} all-to-all(f32[16,24,256]{2,1,0:T(8,128)S(1)} %maximum_maximum_fusion.1), channel_id=1, replica_groups=mesh['x'=4,'z'=8,'c'=2,'y'=4] {'z','c'}, dimensions={0} | all-to-all | bytes 786432 | tf_op jit(solution)/shard_map/curvature/all_to_all | solution.py:187
  122.5 17.2 %all_to_all.70 = f32[16,48,256]{2,1,0:T(8,128)S(1)} all-to-all(f32[16,48,256]{2,1,0:T(8,128)S(1)} %broadcast_in_dim.46), channel_id=1, replica_groups=mesh['x'=4,'z'=8,'c'=2,'y'=4] {'x','y'}, dimensions={0} | all-to-all | bytes 1572864 | tf_op jit(solution)/shard_map/curvature/all_to_all | solution.py:192
  140.1 0.7 collective-permute-start
  140.8 0.7 broadcast_in_dim.47
  141.6 3.6 %all-to-all-start.8 = ((f32[16,16,256]{2,1,0:T(8,128)}), f32[16,16,256]{2,1,0:T(8,128)S(1)}, u32[]{:S(2)}, u32[]{:S(2)}) async-start(f32[16,16,256]{2,1,0:T(8,128)} %broadcast_in_dim.47), calls=%async_computation.8 | async-start | bytes 524288 | tf_op jit(solution)/shard_map/curvature/all_to_all | solution.py:134
  145.2 11.5 %all-to-all-done.8 = f32[16,16,256]{2,1,0:T(8,128)S(1)} async-done(((f32[16,16,256]{2,1,0:T(8,128)}), f32[16,16,256]{2,1,0:T(8,128)S(1)}, u32[]{:S(2)}, u32[]{:S(2)}) %all-to-all-start.8) | async-done | bytes 262176 | tf_op jit(solution)/shard_map/curvature/all_to_all | solution.py:134
  156.8 15.9 %solve.1 = f32[256,256]{1,0:T(8,128)S(1)} custom-call(f32[256,256]{1,0:T(8,128)S(1)} %bitcast.25, f32[256,256]{1,0:T(8,128)S(1)} %slice.24.x_ref), custom_call_target="tpu_custom_call" | custom-call | flops 67108864 | bytes 786432 | tf_op jit(solution)/shard_map/solve/solve/pallas_call | solution.py:106
  173.1 0.8 maximum_bitcast_fusion
  175.2 1.6 fusion.3
  (33 shorter events, 4.0 us)
Async XLA Ops:
  0.0 1.0 copy-start
  48.8 15.6 %all-to-all-start.3 = ((bf16[32,32,256]{2,1,0:T(8,128)(2,1)}), bf16[32,32,256]{2,1,0:T(8,128)(2,1)S(1)}, u32[]{:S(2)}, u32[]{:S(2)}) async-start(bf16[32,32,256]{2,1,0:T(8,128)(2,1)} %broadcast_in_dim.18), calls=%async_computation.3 | async-start | bytes 1048576 | tf_op jit(solution)/shard_map/raw_basis/all_to_all | solution.py:134
  79.1 1.6 copy-start.1
  82.1 19.1 %all-to-all-start.5 = ((f32[4,264,256]{2,1,0:T(8,128)}), f32[4,264,256]{2,1,0:T(8,128)S(1)}, u32[]{:S(2)}, u32[]{:S(2)}) async-start(f32[4,264,256]{2,1,0:T(8,128)} %maximum_maximum_fusion), calls=%async_computation.5 | async-start | bytes 2162688 | tf_op jit(solution)/shard_map/coords/all_to_all | solution.py:166
  140.1 32.6 %collective-permute-start = (f32[4,4,8,2,1,2,256]{6,5,3,2,1,0,4:T(2,128)S(1)}, f32[4,4,8,2,1,2,256]{6,5,3,2,1,0,4:T(2,128)S(1)}, u32[]{:S(2)}, u32[]{:S(2)}) collective-permute-start(f32[4,4,8,2,1,2,256]{6,5,3,2,1,0,4:T(2,128)S(1)} %reshape.59), channel_id=1, source_target_pairs={{0,4},{4,0},{1,5},{5,1},{2,6},{6,2},{3,7},{7,3},{8,12},{12,8},{9,1... | collective-permute-start | bytes 1572872 | tf_op jit(solution)/shard_map/solve/ppermute | solution.py:199
  141.6 15.2 %all-to-all-start.8 = ((f32[16,16,256]{2,1,0:T(8,128)}), f32[16,16,256]{2,1,0:T(8,128)S(1)}, u32[]{:S(2)}, u32[]{:S(2)}) async-start(f32[16,16,256]{2,1,0:T(8,128)} %broadcast_in_dim.47), calls=%async_computation.8 | async-start | bytes 524288 | tf_op jit(solution)/shard_map/curvature/all_to_all | solution.py:134
